TPU v7x, 32 devices: a whole 2x2x4 slice. The times are simulated.
32 devices in a mesh: region: 2 (over core), shard: 16 (over z, y, x).
Axes of the slice: x: 2, y: 2, z: 4, core: 2. Of those that a mesh axis runs over, the one named last changes fastest.
Arguments:
- points: bfloat16 [3072, 8, 128], P(('region', 'shard')), may hold values from -12 to 12
- block_owner: int32 [3072, 1], P(('region', 'shard')), may hold values from 0 to 15; in each aligned block of 96 rows (0 to 95, 96 to 191, ...) at most 12 rows name the same one
- block_node: int32 [3072], P(('region', 'shard')), may hold values from 0 to 1
- queries: bfloat16 [8192, 128], P(('region', 'shard')), may hold values from -240 to 240
- w_in: bfloat16 [128, 768], replicated, may hold values from -0.5 to 0.5
- w_key: bfloat16 [768, 768], replicated, may hold values from -0.21875 to 0.21875
- w_value: bfloat16 [768, 768], replicated, may hold values from -0.21875 to 0.21875
- w_query: bfloat16 [128, 768], replicated, may hold values from -0.5 to 0.5
- w_out: bfloat16 [768, 128], replicated, may hold values from -0.21875 to 0.21875
Outputs:
- readout: bfloat16 [8192, 128], P(('region', 'shard'))
Inputs may be any that keep to these rules, and one draw needn't show every extreme that they name: `block_owner`: among the 96 blocks of one device no shard is named more than 12 times, and some device names one shard exactly 12 times.
All inputs are finite; a program needn't handle non-finite values.
Results may differ from a plain program's by a relative error of at most 0.018.
Values may be sent and summed in bfloat16 or wider, within the bound.
A program may use at most 64 MiB of HBM per device.

v0:
```python
import functools

import jax
import jax.numpy as jnp
from jax import lax
from jax.experimental import pallas as pl
from jax.experimental.pallas import tpu as pltpu
from jax.sharding import PartitionSpec as P

HEADS = 12
HEAD_DIM = 64
S_DEV = 2
LANES = 128
ROWS = 16
MESH = pl.DeviceIdType.MESH
F32 = jnp.float32
BF16 = jnp.bfloat16


def dot(a, b, dims=((1,), (0,))):
    return lax.dot_general(a, b, (dims, ((), ())), preferred_element_type=F32)


def iota(shape, axis):
    return lax.broadcasted_iota(jnp.int32, shape, axis)


def each(count, do):
    if count <= 32:
        for k in range(count):
            do(k)
    else:
        lax.fori_loop(0, count, lambda k, c: (do(k), c)[1], 0)


def kernel(
    regions, shards,
    points_hbm, owner_ref, node_ref, queries_hbm, w_in_hbm, w_key_hbm, w_value_hbm, w_query_hbm, w_out_hbm,
    out_ref,
    points, queries, w_in, w_key, w_value, w_query, w_out,
    send1, recv1, send2, recv2, query_t, fold, in_sem, send1_sem, recv1_sem, send2_sem, recv2_sem,
):
    devices = regions * shards
    point_rows, _ = points.shape
    width = w_in.shape[1]
    chunks = width // LANES
    blocks = owner_ref.shape[1]
    region = lax.axis_index("region")
    shard = lax.axis_index("shard")
    me = region * shards + shard

    barrier = pltpu.get_barrier_semaphore()

    def peer(k):
        other = lax.rem(me + k + 1, devices)
        return (other // shards, lax.rem(other, shards))

    loads = [
        pltpu.make_async_copy(src, dst, in_sem.at[k])
        for k, (src, dst) in enumerate((
            (points_hbm, points), (w_in_hbm, w_in), (queries_hbm, queries), (w_query_hbm, w_query),
            (w_out_hbm, w_out), (w_value_hbm, w_value), (w_key_hbm, w_key),
        ))
    ]
    for load in loads:
        load.start()

    def greet(k):
        pl.semaphore_signal(barrier, inc=1, device_id=peer(k), device_id_type=MESH)

    each(devices - 1, greet)

    ids = owner_ref[...] * S_DEV + node_ref[...]
    assign = (iota((S_DEV * shards, blocks), 0) == ids).astype(BF16)
    per_block = point_rows // blocks
    expand = (iota((blocks, point_rows), 1) // per_block == iota((blocks, point_rows), 0)).astype(BF16)
    assign = dot(assign, expand).astype(BF16)

    loads[0].wait()
    loads[1].wait()
    message = jax.nn.gelu(dot(points[...], w_in[...])).astype(BF16)
    partial = dot(assign, message).astype(BF16)
    stacked = jnp.concatenate([partial[:, j * LANES:(j + 1) * LANES] for j in range(chunks)], axis=0)
    place_shape = (shards * ROWS, chunks * S_DEV * shards)
    row, col = iota(place_shape, 0), iota(place_shape, 1)
    inner = row % ROWS
    wanted = (inner // S_DEV) * (S_DEV * shards) + (row // ROWS) * S_DEV + inner % S_DEV
    place = ((wanted == col) & (inner < chunks * S_DEV)).astype(BF16)
    send1[...] = dot(place, stacked).astype(BF16)

    pl.semaphore_wait(barrier, devices - 1)

    def tile(index):
        return pl.ds(pl.multiple_of(index * ROWS, ROWS), ROWS)

    own1 = pltpu.make_async_copy(send1.at[tile(shard)], recv1.at[tile(shard)], recv1_sem)
    own1.start()

    def scatter(k):
        to = lax.rem(shard + k + 1, shards)
        pltpu.make_async_remote_copy(
            src_ref=send1.at[tile(to)], dst_ref=recv1.at[tile(shard)],
            send_sem=send1_sem, recv_sem=recv1_sem, device_id=(region, to), device_id_type=MESH,
        ).start()

    each(shards - 1, scatter)

    loads[2].wait()
    loads[3].wait()
    query_t[...] = (dot(w_query[...], queries[...], ((0,), (1,))) * HEAD_DIM ** (-0.5)).astype(BF16)
    loads[4].wait()
    loads[5].wait()

    def fold_heads():
        for h in range(HEADS):
            head = slice(h * HEAD_DIM, (h + 1) * HEAD_DIM)
            fold[:, h * LANES:(h + 1) * LANES] = dot(w_value[:, head], w_out[head, :]).astype(BF16)

    fold_heads()

    pltpu.make_async_copy(recv1, recv1, recv1_sem).wait()
    total = recv1[0:ROWS, :].astype(F32)
    for s in range(1, shards):
        total = total + recv1[s * ROWS:(s + 1) * ROWS, :].astype(F32)

    inner = iota((ROWS, LANES), 0)
    real = inner < chunks * S_DEV

    def node_mean(x):
        sums = jnp.sum(x, axis=1, keepdims=True)
        which = iota((ROWS, 1), 0) % S_DEV
        mean = jnp.zeros((ROWS, 1), F32)
        for i in range(S_DEV):
            part = jnp.sum(jnp.where(which == i, sums, 0.0), axis=0, keepdims=True)
            mean = jnp.where(which == i, part, mean)
        return mean * (1.0 / width)

    centred = jnp.where(real, total - node_mean(total), 0.0)
    spread = node_mean(centred * centred)
    send2[...] = (centred * lax.rsqrt(spread + 1e-05)).astype(BF16)

    own2 = pltpu.make_async_copy(send2, recv2.at[tile(me)], recv2_sem)
    own2.start()

    def spread_out(k):
        pltpu.make_async_remote_copy(
            src_ref=send2, dst_ref=recv2.at[tile(me)],
            send_sem=send2_sem, recv_sem=recv2_sem, device_id=peer(k), device_id_type=MESH,
        ).start()

    each(devices - 1, spread_out)

    group_devices = LANES // 2 // S_DEV
    anchors = group_devices * S_DEV
    heads_of = 256 // HEAD_DIM
    pick_shape = (chunks * anchors, group_devices * ROWS)
    row, col = iota(pick_shape, 0), iota(pick_shape, 1)
    anchor = row % anchors
    pick = ((anchor // S_DEV) * ROWS + (row // anchors) * S_DEV + anchor % S_DEV == col).astype(BF16)
    diag_shape = (heads_of * anchors, heads_of * HEAD_DIM)
    diagonal = iota(diag_shape, 0) // anchors == iota(diag_shape, 1) // HEAD_DIM
    loads[6].wait()

    pltpu.make_async_copy(recv2, recv2, recv2_sem).wait()
    keys, folded = [], []
    for c in range(devices // group_devices):
        rows = recv2[c * group_devices * ROWS:(c + 1) * group_devices * ROWS, :]
        picked = dot(pick, rows).astype(BF16)
        normed = jnp.concatenate([picked[j * anchors:(j + 1) * anchors] for j in range(chunks)], axis=1)
        keys.append(dot(normed, w_key[...]).astype(BF16))
        folded.append(dot(normed, fold[...]))

    readout_t = jnp.zeros((LANES, queries.shape[0]), F32)
    for g in range(HEADS // heads_of):
        features = slice(g * 256, (g + 1) * 256)
        scores = []
        for key in keys:
            block = jnp.where(diagonal, jnp.concatenate([key[:, features]] * heads_of, axis=0), jnp.zeros((), BF16))
            scores.append(dot(block, query_t[features, :]))
        expos = [[] for _ in keys]
        for h in range(heads_of):
            head = [s[h * anchors:(h + 1) * anchors] for s in scores]
            peak = functools.reduce(jnp.maximum, [jnp.max(s, axis=0, keepdims=True) for s in head])
            expo = [jnp.exp(s - peak) for s in head]
            scale = 1.0 / sum(jnp.sum(e, axis=0, keepdims=True) for e in expo)
            for c, e in enumerate(expo):
                expos[c].append((e * scale).astype(BF16))
        for c, value in enumerate(folded):
            weights = jnp.concatenate(expos[c], axis=0)
            value = jnp.concatenate(
                [value[:, h * LANES:(h + 1) * LANES] for h in range(g * heads_of, (g + 1) * heads_of)], axis=0
            )
            readout_t = readout_t + dot(value.T.astype(BF16), weights)
    out_ref[...] = readout_t.T.astype(BF16)

    sent1 = send1.at[pl.ds(0, (shards - 1) * ROWS)]
    pltpu.make_async_copy(sent1, sent1, send1_sem).wait()
    sent2 = recv2.at[pl.ds(0, (devices - 1) * ROWS)]
    pltpu.make_async_copy(sent2, sent2, send2_sem).wait()


def body(regions, shards, points, block_owner, block_node, queries, w_in, w_key, w_value, w_query, w_out):
    blocks, per_block, features = points.shape
    points = points.reshape(blocks * per_block, features)
    owner = block_owner.reshape(1, blocks)
    node = block_node.reshape(1, blocks)
    width = w_in.shape[1]
    hbm = pl.BlockSpec(memory_space=pl.ANY)
    vmem = pl.BlockSpec(memory_space=pltpu.VMEM)
    devices = regions * shards
    local = [points, queries, w_in, w_key, w_value, w_query, w_out]
    return pl.pallas_call(
        functools.partial(kernel, regions, shards),
        out_shape=jax.ShapeDtypeStruct((queries.shape[0], w_out.shape[1]), BF16),
        in_specs=[hbm, vmem, vmem] + [hbm] * 6,
        out_specs=vmem,
        scratch_shapes=[pltpu.VMEM(x.shape, x.dtype) for x in local] + [
            pltpu.VMEM((shards * ROWS, LANES), BF16),
            pltpu.VMEM((shards * ROWS, LANES), BF16),
            pltpu.VMEM((ROWS, LANES), BF16),
            pltpu.VMEM((devices * ROWS, LANES), BF16),
            pltpu.VMEM((width, queries.shape[0]), BF16),
            pltpu.VMEM((width, HEADS * LANES), BF16),
            pltpu.SemaphoreType.DMA((7,)),
            pltpu.SemaphoreType.DMA,
            pltpu.SemaphoreType.DMA,
            pltpu.SemaphoreType.DMA,
            pltpu.SemaphoreType.DMA,
        ],
        compiler_params=pltpu.CompilerParams(
            collective_id=0, has_side_effects=True, vmem_limit_bytes=48 * 1024 * 1024
        ),
    )(points, owner, node, queries, w_in, w_key, w_value, w_query, w_out)


def solution(mesh):
    both = ("region", "shard")
    return jax.shard_map(
        functools.partial(body, mesh.shape["region"], mesh.shape["shard"]),
        mesh=mesh,
        in_specs=(P(both, None, None), P(both, None), P(both), P(both, None), P(), P(), P(), P(), P()),
        out_specs=P(both, None),
        check_vma=False,
    )
```

profile of v0, /device:TPU:0, one launch (start us, length us, event | category | flops | bytes accessed | tf_op | source)
XLA Modules:
  0.0 29.4 jit_solution(11065112540854508459)
XLA Ops:
  0.0 0.0 copy-start
  0.0 1.3 %copy-done = bf16[768,768]{1,0:T(8,128)(2,1)S(1)} copy-done((bf16[768,768]{1,0:T(8,128)(2,1)S(1)}, bf16[768,768]{1,0:T(8,128)(2,1)}, u32[]{:S(2)}) %copy-start) | copy-done | bytes 1179672
  1.3 0.0 copy-start.1
  1.3 1.3 %copy-done.1 = bf16[768,768]{1,0:T(8,128)(2,1)S(1)} copy-done((bf16[768,768]{1,0:T(8,128)(2,1)S(1)}, bf16[768,768]{1,0:T(8,128)(2,1)}, u32[]{:S(2)}) %copy-start.1) | copy-done | bytes 1179672
  2.5 0.0 copy-start.2
  2.5 0.9 %copy-done.2 = bf16[96,8,128]{2,1,0:T(8,128)(2,1)S(1)} copy-done((bf16[96,8,128]{2,1,0:T(8,128)(2,1)S(1)}, bf16[96,8,128]{2,1,0:T(8,128)(2,1)}, u32[]{:S(2)}) %copy-start.2) | copy-done | bytes 196632
  3.5 0.0 copy-start.3
  3.5 0.9 %copy-done.3 = bf16[128,768]{1,0:T(8,128)(2,1)S(1)} copy-done((bf16[128,768]{1,0:T(8,128)(2,1)S(1)}, bf16[128,768]{1,0:T(8,128)(2,1)}, u32[]{:S(2)}) %copy-start.3) | copy-done | bytes 196632
  4.4 0.0 copy-start.4
  4.4 0.9 %copy-done.4 = bf16[128,768]{1,0:T(8,128)(2,1)S(1)} copy-done((bf16[128,768]{1,0:T(8,128)(2,1)S(1)}, bf16[128,768]{1,0:T(8,128)(2,1)}, u32[]{:S(2)}) %copy-start.4) | copy-done | bytes 196632
  5.3 0.0 copy-start.5
  5.3 0.9 %copy-done.5 = bf16[768,128]{1,0:T(8,128)(2,1)S(1)} copy-done((bf16[768,128]{1,0:T(8,128)(2,1)S(1)}, bf16[768,128]{1,0:T(8,128)(2,1)}, u32[]{:S(2)}) %copy-start.5) | copy-done | bytes 196632
  6.3 0.0 copy-start.6
  6.3 0.8 %copy-done.6 = bf16[256,128]{1,0:T(8,128)(2,1)S(1)} copy-done((bf16[256,128]{1,0:T(8,128)(2,1)S(1)}, bf16[256,128]{1,0:T(8,128)(2,1)}, u32[]{:S(2)}) %copy-start.6) | copy-done | bytes 65560
  7.1 0.0 copy-start.7
  7.1 0.7 %copy-done.7 = s32[96,1]{0,1:T(1,128)S(1)} copy-done((s32[96,1]{0,1:T(1,128)S(1)}, s32[96,1]{0,1:T(1,128)}, u32[]{:S(2)}) %copy-start.7) | copy-done | bytes 408
  7.7 0.0 copy-start.8
  7.8 0.7 %copy-done.8 = s32[96]{0:T(128)S(1)} copy-done((s32[96]{0:T(128)S(1)}, s32[96]{0:T(128)}, u32[]{:S(2)}) %copy-start.8) | copy-done | bytes 408
  8.4 20.4 %shard_map.91 = bf16[256,128]{1,0:T(8,128)(2,1)S(1)} custom-call(bf16[768,128]{1,0:T(8,128)(2,1)S(1)} %bitcast.3, s32[1,96]{1,0:T(1,128)S(1)} %bitcast.4, s32[1,96]{1,0:T(1,128)S(1)} %bitcast.5, bf16[256,128]{1,0:T(8,128)(2,1)S(1)} %copy-done.6, bf16[128,768]{1,0:T(8,128)(2,1)S(1)} %copy-done.3, bf16[768,768]{1,0:T(8,128)(2,1)S(1)} %copy-done, ...), custom_call_target="tpu_custom_call" | custom-call | tf_op jit(solution)/shard_map/pallas_call | solution.py:212
  28.8 0.6 %copy.11 = bf16[256,128]{1,0:T(8,128)(2,1)} copy(bf16[256,128]{1,0:T(8,128)(2,1)S(1)} %shard_map.91) | data formatting | bytes 131072
Async XLA Ops:
  0.0 1.3 %copy-start = (bf16[768,768]{1,0:T(8,128)(2,1)S(1)}, bf16[768,768]{1,0:T(8,128)(2,1)}, u32[]{:S(2)}) copy-start(bf16[768,768]{1,0:T(8,128)(2,1)} %w_key_hbm.1) | copy-start | bytes 3538948
  1.3 1.3 %copy-start.1 = (bf16[768,768]{1,0:T(8,128)(2,1)S(1)}, bf16[768,768]{1,0:T(8,128)(2,1)}, u32[]{:S(2)}) copy-start(bf16[768,768]{1,0:T(8,128)(2,1)} %w_value_hbm.1) | copy-start | bytes 3538948
  2.5 0.9 %copy-start.2 = (bf16[96,8,128]{2,1,0:T(8,128)(2,1)S(1)}, bf16[96,8,128]{2,1,0:T(8,128)(2,1)}, u32[]{:S(2)}) copy-start(bf16[96,8,128]{2,1,0:T(8,128)(2,1)} %param.9) | copy-start | bytes 589828
  3.5 0.9 %copy-start.3 = (bf16[128,768]{1,0:T(8,128)(2,1)S(1)}, bf16[128,768]{1,0:T(8,128)(2,1)}, u32[]{:S(2)}) copy-start(bf16[128,768]{1,0:T(8,128)(2,1)} %w_in_hbm.1) | copy-start | bytes 589828
  4.4 0.9 %copy-start.4 = (bf16[128,768]{1,0:T(8,128)(2,1)S(1)}, bf16[128,768]{1,0:T(8,128)(2,1)}, u32[]{:S(2)}) copy-start(bf16[128,768]{1,0:T(8,128)(2,1)} %w_query_hbm.1) | copy-start | bytes 589828
  5.3 0.9 %copy-start.5 = (bf16[768,128]{1,0:T(8,128)(2,1)S(1)}, bf16[768,128]{1,0:T(8,128)(2,1)}, u32[]{:S(2)}) copy-start(bf16[768,128]{1,0:T(8,128)(2,1)} %w_out_hbm.1) | copy-start | bytes 589828
  6.3 0.8 %copy-start.6 = (bf16[256,128]{1,0:T(8,128)(2,1)S(1)}, bf16[256,128]{1,0:T(8,128)(2,1)}, u32[]{:S(2)}) copy-start(bf16[256,128]{1,0:T(8,128)(2,1)} %queries_hbm.1) | copy-start | bytes 196612
  7.1 0.7 %copy-start.7 = (s32[96,1]{0,1:T(1,128)S(1)}, s32[96,1]{0,1:T(1,128)}, u32[]{:S(2)}) copy-start(s32[96,1]{0,1:T(1,128)} %param.10) | copy-start | bytes 1156
  7.7 0.7 %copy-start.8 = (s32[96]{0:T(128)S(1)}, s32[96]{0:T(128)}, u32[]{:S(2)}) copy-start(s32[96]{0:T(128)} %param.11) | copy-start | bytes 1156
where the time goes:
time: 29.8 us; the launch traced here: 29.4 us
  Pallas kernels  20.4 us (68%)
  local copies, waits for them, and re-layouts  9.03 us (30%)
    pallas_call x1, Pallas kernels, body(): pl.pallas_call(functools.partial(kernel, regions, shards), out_shape=jax....  20.4 us
    unnamed x19, local copies, waits for them, and re-layouts  9.03 us

commit v1 on v0

v1 whole, which is shorter than its diff:
```python
import functools

import jax
import jax.numpy as jnp
from jax import lax
from jax.experimental import pallas as pl
from jax.experimental.pallas import tpu as pltpu
from jax.sharding import PartitionSpec as P

HEADS = 12
HEAD_DIM = 64
S_DEV = 2
LANES = 128
ROWS = 16
VMEM_BYTES = 64 * 1024 * 1024 - 96 * 1024
MESH = pl.DeviceIdType.MESH
F32 = jnp.float32
BF16 = jnp.bfloat16


def dot(a, b, dims=((1,), (0,))):
    return lax.dot_general(a, b, (dims, ((), ())), preferred_element_type=F32)


def iota(shape, axis):
    return lax.broadcasted_iota(jnp.int32, shape, axis)


def selection(rows, cols, wanted, real=None):
    row = iota((rows, LANES), 0)
    lane = iota((rows, LANES), 1)
    column = wanted(row)
    if real is not None:
        column = jnp.where(real(row), column, -1)
    parts = [(column == lane + start).astype(BF16) for start in range(0, cols, LANES)]
    return jnp.concatenate(parts, axis=1)[:, :cols]


def div(x, by):
    return lax.shift_right_logical(x, by.bit_length() - 1) if by & (by - 1) == 0 else x // by


def mod(x, by):
    return x & (by - 1) if by & (by - 1) == 0 else x % by


def each(count, do):
    if count <= 32:
        for k in range(count):
            do(k)
    else:
        lax.fori_loop(0, count, lambda k, c: (do(k), c)[1], 0)


def kernel(
    regions, shards,
    points_hbm, owner_hbm, node_hbm, queries_hbm, w_in_hbm, w_key_hbm, w_value_hbm, w_query_hbm, w_out_hbm,
    out_ref,
    points, owner_ref, node_ref, queries, w_in, w_key, w_value, w_query, w_out,
    send1, recv1, send2, recv2, recv3, query_t, fold, in_sem, send1_sem, recv1_sem, send2_sem, recv2_sem, send3_sem, recv3_sem,
):
    devices = regions * shards
    point_rows, _ = points.shape
    width = w_in.shape[1]
    chunks = width // LANES
    blocks = owner_ref.shape[1]
    region = lax.axis_index("region")
    shard = lax.axis_index("shard")
    me = region * shards + shard

    barrier = pltpu.get_barrier_semaphore()

    def peer(k):
        other = lax.rem(me + k + 1, devices)
        return (other // shards, lax.rem(other, shards))

    loads = [
        pltpu.make_async_copy(src, dst, in_sem.at[k])
        for k, (src, dst) in enumerate((
            (points_hbm, points), (w_in_hbm, w_in), (queries_hbm, queries), (w_query_hbm, w_query),
            (w_out_hbm, w_out), (w_value_hbm, w_value), (w_key_hbm, w_key), (owner_hbm, owner_ref), (node_hbm, node_ref),
        ))
    ]
    for load in loads:
        load.start()

    def greet(k):
        pl.semaphore_signal(barrier, inc=1, device_id=peer(k), device_id_type=MESH)

    each(devices - 1, greet)

    loads[7].wait()
    loads[8].wait()
    ids = owner_ref[...] * S_DEV + node_ref[...]
    assign = (iota((S_DEV * shards, blocks), 0) == ids).astype(BF16)
    per_block = point_rows // blocks
    expand = (div(iota((blocks, point_rows), 1), per_block) == iota((blocks, point_rows), 0)).astype(BF16)
    assign = dot(assign, expand).astype(BF16)

    loads[0].wait()
    loads[1].wait()
    message = jax.nn.gelu(dot(points[...], w_in[...])).astype(BF16)
    partial = dot(assign, message).astype(BF16)
    stacked = jnp.concatenate([partial[:, j * LANES:(j + 1) * LANES] for j in range(chunks)], axis=0)
    place = selection(
        shards * ROWS, chunks * S_DEV * shards,
        lambda row: div(mod(row, ROWS), S_DEV) * (S_DEV * shards) + div(row, ROWS) * S_DEV + mod(row, S_DEV),
        lambda row: mod(row, ROWS) < chunks * S_DEV,
    )
    send1[...] = dot(place, stacked).astype(BF16)

    pl.semaphore_wait(barrier, devices - 1)

    def tile(index):
        return pl.ds(pl.multiple_of(index * ROWS, ROWS), ROWS)

    own1 = pltpu.make_async_copy(send1.at[tile(shard)], recv1.at[tile(shard)], recv1_sem)
    own1.start()

    def scatter(k):
        to = lax.rem(shard + k + 1, shards)
        pltpu.make_async_remote_copy(
            src_ref=send1.at[tile(to)], dst_ref=recv1.at[tile(shard)],
            send_sem=send1_sem, recv_sem=recv1_sem, device_id=(region, to), device_id_type=MESH,
        ).start()

    each(shards - 1, scatter)

    loads[2].wait()
    loads[3].wait()
    query_t[...] = (dot(w_query[...], queries[...], ((0,), (1,))) * HEAD_DIM ** (-0.5)).astype(BF16)
    group_devices = ROWS
    anchors = group_devices * S_DEV
    heads_of = 256 // HEAD_DIM
    pick = selection(
        chunks * anchors, group_devices * ROWS,
        lambda row: div(mod(row, anchors), S_DEV) * ROWS + div(row, anchors) * S_DEV + mod(row, S_DEV),
    )
    diag_shape = (heads_of * anchors, heads_of * HEAD_DIM)
    diagonal = div(iota(diag_shape, 0), anchors) == div(iota(diag_shape, 1), HEAD_DIM)
    pltpu.make_async_copy(recv1, recv1, recv1_sem).wait()
    total = recv1[0:ROWS, :].astype(F32)
    for s in range(1, shards):
        total = total + recv1[s * ROWS:(s + 1) * ROWS, :].astype(F32)

    inner = iota((ROWS, LANES), 0)
    real = inner < chunks * S_DEV

    def node_mean(x):
        sums = jnp.sum(x, axis=1, keepdims=True)
        which = mod(iota((ROWS, 1), 0), S_DEV)
        mean = jnp.zeros((ROWS, 1), F32)
        for i in range(S_DEV):
            part = jnp.sum(jnp.where(which == i, sums, 0.0), axis=0, keepdims=True)
            mean = jnp.where(which == i, part, mean)
        return mean * (1.0 / width)

    centred = jnp.where(real, total - node_mean(total), 0.0)
    spread = node_mean(centred * centred)
    send2[...] = (centred * lax.rsqrt(spread + 1e-05)).astype(BF16)

    own2 = pltpu.make_async_copy(send2, recv2.at[tile(shard)], recv2_sem)
    own2.start()

    def spread_out(k):
        to = lax.rem(shard + k + 1, shards)
        pltpu.make_async_remote_copy(
            src_ref=send2, dst_ref=recv2.at[tile(shard)],
            send_sem=send2_sem, recv_sem=recv2_sem, device_id=(region, to), device_id_type=MESH,
        ).start()

    each(shards - 1, spread_out)

    loads[4].wait()
    loads[5].wait()

    def fold_heads():
        for h in range(HEADS):
            head = slice(h * HEAD_DIM, (h + 1) * HEAD_DIM)
            fold[:, h * LANES:(h + 1) * LANES] = dot(w_value[:, head], w_out[head, :]).astype(BF16)

    fold_heads()

    loads[6].wait()
    pltpu.make_async_copy(recv2, recv2, recv2_sem).wait()

    def pass_on(k):
        slot = pl.ds(k * shards * ROWS, shards * ROWS)
        pltpu.make_async_remote_copy(
            src_ref=recv2, dst_ref=recv3.at[slot],
            send_sem=send3_sem, recv_sem=recv3_sem,
            device_id=(lax.rem(region + k + 1, regions), shard), device_id_type=MESH,
        ).start()

    each(regions - 1, pass_on)

    keys, folded = [], []

    def project(source):
        for start in range(0, source.shape[0], group_devices * ROWS):
            picked = dot(pick, source[start:start + group_devices * ROWS, :]).astype(BF16)
            normed = jnp.concatenate([picked[j * anchors:(j + 1) * anchors] for j in range(chunks)], axis=1)
            keys.append(dot(normed, w_key[...]).astype(BF16))
            folded.append(dot(normed, fold[...]))

    project(recv2)
    pltpu.make_async_copy(recv3, recv3, recv3_sem).wait()
    project(recv3)

    readout_t = jnp.zeros((LANES, queries.shape[0]), F32)
    for g in range(HEADS // heads_of):
        features = slice(g * 256, (g + 1) * 256)
        scores = []
        for key in keys:
            block = jnp.where(diagonal, jnp.concatenate([key[:, features]] * heads_of, axis=0), jnp.zeros((), BF16))
            scores.append(dot(block, query_t[features, :]))
        expos = [[] for _ in keys]
        for h in range(heads_of):
            head = [s[h * anchors:(h + 1) * anchors] for s in scores]
            peak = functools.reduce(jnp.maximum, [jnp.max(s, axis=0, keepdims=True) for s in head])
            expo = [jnp.exp(s - peak) for s in head]
            scale = 1.0 / sum(jnp.sum(e, axis=0, keepdims=True) for e in expo)
            for c, e in enumerate(expo):
                expos[c].append((e * scale).astype(BF16))
        weights = jnp.concatenate([e for part in expos for e in part], axis=0)
        values = jnp.concatenate(
            [value[:, h * LANES:(h + 1) * LANES] for value in folded for h in range(g * heads_of, (g + 1) * heads_of)],
            axis=0,
        )
        readout_t = readout_t + dot(values.T.astype(BF16), weights)
    out_ref[...] = readout_t.T.astype(BF16)

    sent1 = send1.at[pl.ds(0, (shards - 1) * ROWS)]
    pltpu.make_async_copy(sent1, sent1, send1_sem).wait()
    sent2 = recv2.at[pl.ds(0, (shards - 1) * ROWS)]
    pltpu.make_async_copy(sent2, sent2, send2_sem).wait()
    pltpu.make_async_copy(recv3, recv3, send3_sem).wait()


def body(regions, shards, points, block_owner, block_node, queries, w_in, w_key, w_value, w_query, w_out):
    blocks, per_block, features = points.shape
    points = points.reshape(blocks * per_block, features)
    owner = block_owner.reshape(1, blocks)
    node = block_node.reshape(1, blocks)
    width = w_in.shape[1]
    hbm = pl.BlockSpec(memory_space=pltpu.HBM)
    vmem = pl.BlockSpec(memory_space=pltpu.VMEM)
    local = [points, owner, node, queries, w_in, w_key, w_value, w_query, w_out]
    return pl.pallas_call(
        functools.partial(kernel, regions, shards),
        out_shape=jax.ShapeDtypeStruct((queries.shape[0], w_out.shape[1]), BF16),
        in_specs=[hbm] * 9,
        out_specs=vmem,
        scratch_shapes=[pltpu.VMEM(x.shape, x.dtype) for x in local] + [
            pltpu.VMEM((shards * ROWS, LANES), BF16),
            pltpu.VMEM((shards * ROWS, LANES), BF16),
            pltpu.VMEM((ROWS, LANES), BF16),
            pltpu.VMEM((shards * ROWS, LANES), BF16),
            pltpu.VMEM(((regions - 1) * shards * ROWS, LANES), BF16),
            pltpu.VMEM((width, queries.shape[0]), BF16),
            pltpu.VMEM((width, HEADS * LANES), BF16),
            pltpu.SemaphoreType.DMA((9,)),
            pltpu.SemaphoreType.DMA,
            pltpu.SemaphoreType.DMA,
            pltpu.SemaphoreType.DMA,
            pltpu.SemaphoreType.DMA,
            pltpu.SemaphoreType.DMA,
            pltpu.SemaphoreType.DMA,
        ],
        compiler_params=pltpu.CompilerParams(
            collective_id=0, has_side_effects=True, vmem_limit_bytes=VMEM_BYTES
        ),
    )(points, owner, node, queries, w_in, w_key, w_value, w_query, w_out)


def solution(mesh):
    both = ("region", "shard")
    return jax.shard_map(
        functools.partial(body, mesh.shape["region"], mesh.shape["shard"]),
        mesh=mesh,
        in_specs=(P(both, None, None), P(both, None), P(both), P(both, None), P(), P(), P(), P(), P()),
        out_specs=P(both, None),
        check_vma=False,
    )
```

time: 29.8 us -> 21.3 us (0.71)
  local copies, waits for them, and re-layouts: 9.03 us -> 1.47 us
  Pallas kernels: 20.4 us -> 19.7 us
    unnamed x19 -> x1, local copies, waits for them, and re-layouts: 9.03 us -> 1.47 us
    pallas_call x1, Pallas kernels: 20.4 us -> 19.7 us  [body(): pl.pallas_call(functools.partial(kernel, regions, shards), out_shape=jax....]
where the time goes in v1:
time: 21.3 us; the launch traced here: 21.2 us
  Pallas kernels  19.7 us (92%)
  local copies, waits for them, and re-layouts  1.47 us (7%)
    pallas_call x1, Pallas kernels, body(): pl.pallas_call(functools.partial(kernel, regions, shards), out_shape=jax....  19.7 us
    unnamed x1, local copies, waits for them, and re-layouts  1.47 us

profile of v1, /device:TPU:0, one launch (start us, length us, event | category | flops | bytes accessed | tf_op | source)
XLA Modules:
  0.0 21.2 jit_solution(10646580358960433092)
XLA Ops:
  0.0 19.7 %shard_map.91 = bf16[256,128]{1,0:T(8,128)(2,1)} custom-call(bf16[768,128]{1,0:T(8,128)(2,1)} %bitcast.3, s32[1,96]{1,0:T(1,128)} %bitcast.4, s32[1,96]{1,0:T(1,128)} %bitcast.5, bf16[256,128]{1,0:T(8,128)(2,1)} %queries_hbm.1, bf16[128,768]{1,0:T(8,128)(2,1)} %w_in_hbm.1, bf16[768,768]{1,0:T(8,128)(2,1)} %w_key_hbm.1, bf16[768,768]{1,0:T(8,128)(2,1)} %w_value_hbm.1, ...), custom_call_target="tpu_custom_call" | custom-call | tf_op jit(solution)/shard_map/pallas_call | solution.py:249
  19.7 1.5 %copy.11 = bf16[256,128]{1,0:T(8,128)(2,1)} copy(bf16[256,128]{1,0:T(8,128)(2,1)} %shard_map.91) | data formatting | bytes 131072

commit v2 on v1

--- a/solution.py
+++ b/solution.py
@@ -59,20 +59,14 @@
     points, owner_ref, node_ref, queries, w_in, w_key, w_value, w_query, w_out,
     send1, recv1, send2, recv2, recv3, query_t, fold, in_sem, send1_sem, recv1_sem, send2_sem, recv2_sem, send3_sem, recv3_sem,
 ):
-    devices = regions * shards
     point_rows, _ = points.shape
     width = w_in.shape[1]
     chunks = width // LANES
     blocks = owner_ref.shape[1]
     region = lax.axis_index("region")
     shard = lax.axis_index("shard")
-    me = region * shards + shard
 
     barrier = pltpu.get_barrier_semaphore()
-
-    def peer(k):
-        other = lax.rem(me + k + 1, devices)
-        return (other // shards, lax.rem(other, shards))
 
     loads = [
         pltpu.make_async_copy(src, dst, in_sem.at[k])
@@ -81,13 +75,21 @@
             (w_out_hbm, w_out), (w_value_hbm, w_value), (w_key_hbm, w_key), (owner_hbm, owner_ref), (node_hbm, node_ref),
         ))
     ]
-    for load in loads:
-        load.start()
+    for k in (7, 8, 0, 1):
+        loads[k].start()
 
     def greet(k):
-        pl.semaphore_signal(barrier, inc=1, device_id=peer(k), device_id_type=MESH)
-
-    each(devices - 1, greet)
+        pl.semaphore_signal(
+            barrier, inc=1, device_id=(region, mod(shard + k + 1, shards)), device_id_type=MESH
+        )
+
+    def greet_region(k):
+        pl.semaphore_signal(
+            barrier, inc=1, device_id=(mod(region + k + 1, regions), shard), device_id_type=MESH
+        )
+
+    each(shards - 1, greet)
+    each(regions - 1, greet_region)
 
     loads[7].wait()
     loads[8].wait()
@@ -99,7 +101,9 @@
 
     loads[0].wait()
     loads[1].wait()
-    message = jax.nn.gelu(dot(points[...], w_in[...])).astype(BF16)
+    for k in (2, 3, 4, 5, 6):
+        loads[k].start()
+    message = jax.nn.gelu(dot(points[...], w_in[...]).astype(BF16))
     partial = dot(assign, message).astype(BF16)
     stacked = jnp.concatenate([partial[:, j * LANES:(j + 1) * LANES] for j in range(chunks)], axis=0)
     place = selection(
@@ -109,7 +113,7 @@
     )
     send1[...] = dot(place, stacked).astype(BF16)
 
-    pl.semaphore_wait(barrier, devices - 1)
+    pl.semaphore_wait(barrier, shards + regions - 2)
 
     def tile(index):
         return pl.ds(pl.multiple_of(index * ROWS, ROWS), ROWS)
@@ -118,7 +122,7 @@
     own1.start()
 
     def scatter(k):
-        to = lax.rem(shard + k + 1, shards)
+        to = mod(shard + k + 1, shards)
         pltpu.make_async_remote_copy(
             src_ref=send1.at[tile(to)], dst_ref=recv1.at[tile(shard)],
             send_sem=send1_sem, recv_sem=recv1_sem, device_id=(region, to), device_id_type=MESH,
@@ -163,7 +167,7 @@
     own2.start()
 
     def spread_out(k):
-        to = lax.rem(shard + k + 1, shards)
+        to = mod(shard + k + 1, shards)
         pltpu.make_async_remote_copy(
             src_ref=send2, dst_ref=recv2.at[tile(shard)],
             send_sem=send2_sem, recv_sem=recv2_sem, device_id=(region, to), device_id_type=MESH,
@@ -189,7 +193,7 @@
         pltpu.make_async_remote_copy(
             src_ref=recv2, dst_ref=recv3.at[slot],
             send_sem=send3_sem, recv_sem=recv3_sem,
-            device_id=(lax.rem(region + k + 1, regions), shard), device_id_type=MESH,
+            device_id=(mod(region + k + 1, regions), shard), device_id_type=MESH,
         ).start()
 
     each(regions - 1, pass_on)

time: 21.3 us -> 21.1 us (level)
  Pallas kernels: 19.7 us -> 19.4 us
    pallas_call x1, Pallas kernels: 19.7 us -> 19.4 us  [body(): pl.pallas_call(functools.partial(kernel, regions, shards), out_shape=jax....]
where the time goes in v2:
time: 21.1 us; the launch traced here: 20.9 us
  Pallas kernels  19.4 us (92%)
  local copies, waits for them, and re-layouts  1.47 us (7%)
    pallas_call x1, Pallas kernels, body(): pl.pallas_call(functools.partial(kernel, regions, shards), out_shape=jax....  19.4 us
    unnamed x1, local copies, waits for them, and re-layouts  1.47 us

profile of v2, /device:TPU:0, one launch (start us, length us, event | category | flops | bytes accessed | tf_op | source)
XLA Modules:
  0.0 20.9 jit_solution(9369963990945534372)
XLA Ops:
  0.0 19.4 %shard_map.91 = bf16[256,128]{1,0:T(8,128)(2,1)} custom-call(bf16[768,128]{1,0:T(8,128)(2,1)} %bitcast.3, s32[1,96]{1,0:T(1,128)} %bitcast.4, s32[1,96]{1,0:T(1,128)} %bitcast.5, bf16[256,128]{1,0:T(8,128)(2,1)} %queries_hbm.1, bf16[128,768]{1,0:T(8,128)(2,1)} %w_in_hbm.1, bf16[768,768]{1,0:T(8,128)(2,1)} %w_key_hbm.1, bf16[768,768]{1,0:T(8,128)(2,1)} %w_value_hbm.1, ...), custom_call_target="tpu_custom_call" | custom-call | tf_op jit(solution)/shard_map/pallas_call | solution.py:253
  19.4 1.5 %copy.11 = bf16[256,128]{1,0:T(8,128)(2,1)} copy(bf16[256,128]{1,0:T(8,128)(2,1)} %shard_map.91) | data formatting | bytes 131072
